TPU v7x, 32 devices: a whole 2x2x4 slice. The times are simulated.
32 devices in a mesh: gx: 8 (over z, y), gy: 4 (over x, core).
Axes of the slice: x: 2, y: 2, z: 4, core: 2. Of those that a mesh axis runs over, the one named last changes fastest.
Arguments:
- psi: float32 [64, 64, 1024], P(None, 'gx', 'gy'), may hold values from -500 to 500
- potential: float32 [64, 1024], P('gx', 'gy'), may hold values from -2 to 0
Outputs:
- orbitals: float32 [64, 64, 1024], P(None, 'gx', 'gy')
All inputs are finite; a program needn't handle non-finite values.
Results may differ from a plain program's by a relative error of at most 0.0003.
Values sent between devices are 32-bit elements; how exact they have to be, the bound alone decides.
A program may use at most 64 MiB of HBM per device.

v0:
```python
import jax
import jax.numpy as jnp
from jax import lax
from jax.sharding import PartitionSpec as P

NZ = 64


COEFS = (-205.0 / 72.0, 8.0 / 5.0, -1.0 / 5.0, 8.0 / 315.0, -1.0 / 560.0)
CENTER = 6.5
HALF_WIDTH = 5.5


def padded(array, sides, width):
    for axis, dim in sides:
        size, length = (lax.axis_size(axis), array.shape[dim])
        up = [(i, (i + 1) % size) for i in range(size)]
        down = [(j, i) for i, j in up]
        last = lax.slice_in_dim(array, length - width, length, axis=dim)
        first = lax.slice_in_dim(array, 0, width, axis=dim)
        before = lax.ppermute(last, axis, up)
        after = lax.ppermute(first, axis, down)
        array = jnp.concatenate([before, array, after], axis=dim)
    return array


def along_third(field, depth_index):
    laplace = 3.0 * COEFS[0] * field
    for distance in range(1, 5):
        forward = jnp.where(
            depth_index < NZ - distance,
            jnp.roll(field, -distance, 2),
            jnp.roll(field, NZ - distance, 2),
        )
        behind = jnp.where(
            depth_index >= distance, jnp.roll(field, distance, 2), jnp.roll(field, distance - NZ, 2)
        )
        laplace = laplace + COEFS[distance] * (forward + behind)
    return laplace


def hamiltonian(field, field_pot, depth_index):
    row_count = field.shape[1]
    lane_count = field.shape[2]
    padded_x = padded(field, (("gx", 1),), 4)
    laplace = along_third(field, depth_index)
    padded_y = padded(field, (("gy", 2),), 4 * NZ)
    for distance in range(1, 5):
        laplace = laplace + COEFS[distance] * (
            padded_x[:, 4 + distance : 4 + distance + row_count]
            + padded_x[:, 4 - distance : 4 - distance + row_count]
        )
        ahead_start = (4 + distance) * NZ
        back_start = (4 - distance) * NZ
        laplace = laplace + COEFS[distance] * (
            padded_y[:, :, ahead_start : ahead_start + lane_count]
            + padded_y[:, :, back_start : back_start + lane_count]
        )
    return -0.5 * laplace + field_pot * field


def orthonormal(matrix, ncount):
    local_gram = jnp.dot(matrix, matrix.T, precision=lax.Precision.HIGHEST) / ncount
    total_gram = lax.psum(local_gram, ("gx", "gy"))
    lower_factor = jnp.linalg.cholesky(total_gram)
    return lax.linalg.triangular_solve(lower_factor, matrix, left_side=True, lower=True)


def on_device(psi, potential):
    orbit_count = psi.shape[0]
    row_count = psi.shape[1]
    lane_count = psi.shape[2]
    field_pot = potential.reshape(1, row_count, lane_count)
    depth_index = lax.broadcasted_iota(jnp.int32, (1, 1, lane_count), 2) % NZ
    level_one = (hamiltonian(psi, field_pot, depth_index) - CENTER * psi) / HALF_WIDTH
    second = (
        2.0 * (hamiltonian(level_one, field_pot, depth_index) - CENTER * level_one) / HALF_WIDTH
        - psi
    )
    filtered = (
        2.0 * (hamiltonian(second, field_pot, depth_index) - CENTER * second) / HALF_WIDTH
        - level_one
    )
    matrix = filtered.reshape(orbit_count, row_count * lane_count)
    ncount = float(row_count * lane_count * lax.axis_size("gx") * lax.axis_size("gy"))
    first_pass = orthonormal(matrix, ncount)
    final_pass = orthonormal(first_pass, ncount)
    return final_pass.reshape(orbit_count, row_count, lane_count)


def solution(mesh):
    in_specs = (P(None, "gx", "gy"), P("gx", "gy"))
    out_specs = P(None, "gx", "gy")
    return jax.shard_map(
        on_device, mesh=mesh, in_specs=in_specs, out_specs=out_specs, check_vma=False
    )
```

profile of v0, /device:TPU:0, one launch (start us, length us, event | category | flops | bytes accessed | tf_op | source)
XLA Modules:
  0.0 175.1 jit_solution(4066687479152342336)
XLA Ops:
  0.5 2.0 %collective-permute-start.2 = (f32[64,8,256]{2,1,0:T(8,128)}, f32[64,8,256]{2,1,0:T(8,128)S(1)}, u32[]{:S(2)}, u32[]{:S(2)}) collective-permute-start(f32[64,8,256]{2,1,0:T(8,128)} %param.5), channel_id=1, source_target_pairs={{1,0},{2,1},{3,2},{0,3},{5,4},{6,5},{7,6},{4,7},{9,8},{10,9},{11,1... | collective-permute-start | bytes 1572872 | tf_op jit(solution)/shard_map/ppermute | solution.py:22
  2.4 1.4 fusion.198
  3.8 5.4 %collective-permute-start = (f32[64,4,256]{2,1,0:T(4,128)S(1)}, f32[64,4,256]{2,1,0:T(4,128)S(1)}, u32[]{:S(2)}, u32[]{:S(2)}) collective-permute-start(f32[64,4,256]{2,1,0:T(4,128)S(1)} %get-tuple-element.112), channel_id=1, source_target_pairs={{4,0},{8,4},{12,8},{16,12},{20,16},{24,20},{28,24},{0,28},{5,1},{9... | collective-permute-start | bytes 786440 | tf_op jit(solution)/shard_map/ppermute | solution.py:22
  12.8 2.0 %collective-permute-done = f32[64,4,256]{2,1,0:T(4,128)S(1)} collective-permute-done((f32[64,4,256]{2,1,0:T(4,128)S(1)}, f32[64,4,256]{2,1,0:T(4,128)S(1)}, u32[]{:S(2)}, u32[]{:S(2)}) %collective-permute-start) | collective-permute-done | bytes 262176 | tf_op jit(solution)/shard_map/ppermute | solution.py:22
  15.1 4.6 %collective-permute-done.1 = f32[64,4,256]{2,1,0:T(4,128)S(1)} collective-permute-done((f32[64,4,256]{2,1,0:T(4,128)S(1)}, f32[64,4,256]{2,1,0:T(4,128)S(1)}, u32[]{:S(2)}, u32[]{:S(2)}) %collective-permute-start.1) | collective-permute-done | bytes 262176 | tf_op jit(solution)/shard_map/ppermute | solution.py:21
  19.7 3.3 %broadcast_multiply_fusion = (f32[64,8,256]{2,1,0:T(8,128)S(1)}, f32[64,8,256]{2,1,0:T(8,128)S(1)}) fusion(f32[64,8,256]{2,1,0:T(8,128)S(1)} %copy-done, f32[8,256]{1,0:T(8,128)S(1)} %copy-done.1, f32[64,8,256]{2,1,0:T(8,128)S(1)} %collective-permute-done.2, f32[64,8,256]{2,1,0:T(8,128)S(1)} %collective-permute-done.3, ...), kind=kLoop, calls=%fused_computation.221 | loop fusion | flops 9306112 | bytes 16525312 | tf_op jit(solution)/shard_map/div | solution.py:75
  26.0 3.4 %collective-permute-start.4 = (f32[64,4,256]{2,1,0:T(4,128)S(1)}, f32[64,4,256]{2,1,0:T(4,128)S(1)}, u32[]{:S(2)}, u32[]{:S(2)}) collective-permute-start(f32[64,4,256]{2,1,0:T(4,128)S(1)} %get-tuple-element.75), channel_id=1, source_target_pairs={{4,0},{8,4},{12,8},{16,12},{20,16},{24,20},{28,24},{0,28},{5,1},{9... | collective-permute-start | bytes 786440 | tf_op jit(solution)/shard_map/ppermute | solution.py:22
  29.9 10.6 %collective-permute-done.4 = f32[64,4,256]{2,1,0:T(4,128)S(1)} collective-permute-done((f32[64,4,256]{2,1,0:T(4,128)S(1)}, f32[64,4,256]{2,1,0:T(4,128)S(1)}, u32[]{:S(2)}, u32[]{:S(2)}) %collective-permute-start.4) | collective-permute-done | bytes 262176 | tf_op jit(solution)/shard_map/ppermute | solution.py:22
  40.5 3.8 %fusion.33 = f32[64,8,256]{2,1,0:T(8,128)S(1)} fusion(f32[64,8,256]{2,1,0:T(8,128)S(1)} %copy-done, f32[64,8,256]{2,1,0:T(8,128)S(1)} %collective-permute-done.7, f32[64,8,256]{2,1,0:T(8,128)S(1)} %get-tuple-element.6, f32[64,8,256]{2,1,0:T(8,128)S(1)} %collective-permute-done.6, f32[64,4,256]{2,1,0:T(4,128)S(1)} %collective-permute-done.5, ...), kind=kLoop, calls=%fused_computation.81 | loop fusion | flops 10747904 | bytes 12068864 | tf_op jit(solution)/shard_map/sub | solution.py:77
  45.6 0.9 collective-permute-start.10
  47.6 3.5 %collective-permute-start.8 = (f32[64,4,256]{2,1,0:T(4,128)S(1)}, f32[64,4,256]{2,1,0:T(4,128)S(1)}, u32[]{:S(2)}, u32[]{:S(2)}) collective-permute-start(f32[64,4,256]{2,1,0:T(4,128)S(1)} %get-tuple-element.41), channel_id=1, source_target_pairs={{4,0},{8,4},{12,8},{16,12},{20,16},{24,20},{28,24},{0,28},{5,1},{9... | collective-permute-start | bytes 786440 | tf_op jit(solution)/shard_map/ppermute | solution.py:22
  51.5 5.9 %collective-permute-done.8 = f32[64,4,256]{2,1,0:T(4,128)S(1)} collective-permute-done((f32[64,4,256]{2,1,0:T(4,128)S(1)}, f32[64,4,256]{2,1,0:T(4,128)S(1)}, u32[]{:S(2)}, u32[]{:S(2)}) %collective-permute-start.8) | collective-permute-done | bytes 262176 | tf_op jit(solution)/shard_map/ppermute | solution.py:22
  57.4 5.4 %collective-permute-done.9 = f32[64,4,256]{2,1,0:T(4,128)S(1)} collective-permute-done((f32[64,4,256]{2,1,0:T(4,128)S(1)}, f32[64,4,256]{2,1,0:T(4,128)S(1)}, u32[]{:S(2)}, u32[]{:S(2)}) %collective-permute-start.9) | collective-permute-done | bytes 262176 | tf_op jit(solution)/shard_map/ppermute | solution.py:21
  62.8 3.7 %fusion.13 = f32[64,8,256]{2,1,0:T(8,128)S(1)} fusion(f32[64,8,256]{2,1,0:T(8,128)S(1)} %collective-permute-done.11, f32[64,8,256]{2,1,0:T(8,128)S(1)} %fusion.33, f32[64,8,256]{2,1,0:T(8,128)S(1)} %collective-permute-done.10, f32[64,4,256]{2,1,0:T(4,128)S(1)} %collective-permute-done.9, f32[64,4,256]{2,1,0:T(4,128)S(1)} %collective-permute-done.8, ...), kind=kLoop, calls=%fused_computation.61 | loop fusion | flops 10878976 | bytes 11544576 | tf_op jit(solution)/shard_map/sub | solution.py:81
  66.6 0.7 fusion
  67.3 39.9 %psum.14 = f32[64,64]{0,1:T(8,128)S(1)} all-reduce(f32[64,64]{0,1:T(8,128)S(1)} %fusion), channel_id=1, replica_groups=mesh['gx'=8,'gy'=4] {'gx','gy'}, use_global_device_ids=true, to_apply=%region_0.1 | all-reduce | flops 4096 | bytes 32768 | tf_op jit(solution)/shard_map/psum | solution.py:64
  107.3 5.8 %cholesky.44 = f32[64,64]{1,0:T(8,128)S(1)} custom-call(f32[64,64]{1,0:T(8,128)S(1)} %fusion.144), custom_call_target="Cholesky" | custom-call | tf_op jit(solution)/shard_map/jit(cholesky)/cholesky | solution.py:65
  113.8 0.7 fusion.137
  114.5 4.9 %custom-call.6 = f32[1,64,64]{1,2,0:T(8,128)S(1)} custom-call(f32[1,64,64]{2,1,0:T(8,128)S(1)} %fusion.137), custom_call_target="InvertDiagBlocksLowerTriangular" | custom-call | tf_op jit(solution)/shard_map/triangular_solve/custom-call.0 | solution.py:66
  120.8 40.6 %psum.15 = f32[64,64]{0,1:T(8,128)S(1)} all-reduce(f32[64,64]{0,1:T(8,128)S(1)} %convolution_multiply_fusion), channel_id=1, replica_groups=mesh['gx'=8,'gy'=4] {'gx','gy'}, use_global_device_ids=true, to_apply=%region_3.6 | all-reduce | flops 4096 | bytes 32768 | tf_op jit(solution)/shard_map/psum | solution.py:64
  161.4 5.8 %cholesky.55 = f32[64,64]{1,0:T(8,128)S(1)} custom-call(f32[64,64]{1,0:T(8,128)S(1)} %fusion.141), custom_call_target="Cholesky" | custom-call | tf_op jit(solution)/shard_map/jit(cholesky)/cholesky | solution.py:65
  168.0 0.7 fusion.138
  168.6 4.9 %custom-call.7 = f32[1,64,64]{1,2,0:T(8,128)S(1)} custom-call(f32[1,64,64]{2,1,0:T(8,128)S(1)} %fusion.138), custom_call_target="InvertDiagBlocksLowerTriangular" | custom-call | tf_op jit(solution)/shard_map/triangular_solve/custom-call.0 | solution.py:66
  174.2 1.0 copy.13
  (89 shorter events, 13.8 us)
Async XLA Ops:
  0.0 9.2 %copy-start = (f32[64,8,256]{2,1,0:T(8,128)S(1)}, f32[64,8,256]{2,1,0:T(8,128)}, u32[]{:S(2)}) copy-start(f32[64,8,256]{2,1,0:T(8,128)} %param.5) | copy-start | bytes 1572868
  0.0 12.6 %collective-permute-start.3 = (f32[64,8,256]{2,1,0:T(8,128)}, f32[64,8,256]{2,1,0:T(8,128)S(1)}, u32[]{:S(2)}, u32[]{:S(2)}) collective-permute-start(f32[64,8,256]{2,1,0:T(8,128)} %param.5), channel_id=1, source_target_pairs={{0,1},{1,2},{2,3},{3,0},{4,5},{5,6},{6,7},{7,4},{8,9},{9,10},{10,1... | collective-permute-start | bytes 1572872 | tf_op jit(solution)/shard_map/ppermute | solution.py:21
  0.5 14.5 %collective-permute-start.2 = (f32[64,8,256]{2,1,0:T(8,128)}, f32[64,8,256]{2,1,0:T(8,128)S(1)}, u32[]{:S(2)}, u32[]{:S(2)}) collective-permute-start(f32[64,8,256]{2,1,0:T(8,128)} %param.5), channel_id=1, source_target_pairs={{1,0},{2,1},{3,2},{0,3},{5,4},{6,5},{7,6},{4,7},{9,8},{10,9},{11,1... | collective-permute-start | bytes 1572872 | tf_op jit(solution)/shard_map/ppermute | solution.py:22
  3.8 11.0 %collective-permute-start = (f32[64,4,256]{2,1,0:T(4,128)S(1)}, f32[64,4,256]{2,1,0:T(4,128)S(1)}, u32[]{:S(2)}, u32[]{:S(2)}) collective-permute-start(f32[64,4,256]{2,1,0:T(4,128)S(1)} %get-tuple-element.112), channel_id=1, source_target_pairs={{4,0},{8,4},{12,8},{16,12},{20,16},{24,20},{28,24},{0,28},{5,1},{9... | collective-permute-start | bytes 786440 | tf_op jit(solution)/shard_map/ppermute | solution.py:22
  9.2 10.5 %collective-permute-start.1 = (f32[64,4,256]{2,1,0:T(4,128)S(1)}, f32[64,4,256]{2,1,0:T(4,128)S(1)}, u32[]{:S(2)}, u32[]{:S(2)}) collective-permute-start(f32[64,4,256]{2,1,0:T(4,128)S(1)} %get-tuple-element.113), channel_id=1, source_target_pairs={{0,4},{4,8},{8,12},{12,16},{16,20},{20,24},{24,28},{28,0},{1,5},{5... | collective-permute-start | bytes 786440 | tf_op jit(solution)/shard_map/ppermute | solution.py:21
  11.6 0.7 copy-start.1
  25.5 15.0 %collective-permute-start.6 = (f32[64,8,256]{2,1,0:T(8,128)S(1)}, f32[64,8,256]{2,1,0:T(8,128)S(1)}, u32[]{:S(2)}, u32[]{:S(2)}) collective-permute-start(f32[64,8,256]{2,1,0:T(8,128)S(1)} %get-tuple-element.6), channel_id=1, source_target_pairs={{1,0},{2,1},{3,2},{0,3},{5,4},{6,5},{7,6},{4,7},{9,8},{10,9},{11,1... | collective-permute-start | bytes 1572872 | tf_op jit(solution)/shard_map/ppermute | solution.py:22
  25.5 14.9 %collective-permute-start.7 = (f32[64,8,256]{2,1,0:T(8,128)S(1)}, f32[64,8,256]{2,1,0:T(8,128)S(1)}, u32[]{:S(2)}, u32[]{:S(2)}) collective-permute-start(f32[64,8,256]{2,1,0:T(8,128)S(1)} %get-tuple-element.6), channel_id=1, source_target_pairs={{0,1},{1,2},{2,3},{3,0},{4,5},{5,6},{6,7},{7,4},{8,9},{9,10},{10,1... | collective-permute-start | bytes 1572872 | tf_op jit(solution)/shard_map/ppermute | solution.py:21
  26.0 14.4 %collective-permute-start.4 = (f32[64,4,256]{2,1,0:T(4,128)S(1)}, f32[64,4,256]{2,1,0:T(4,128)S(1)}, u32[]{:S(2)}, u32[]{:S(2)}) collective-permute-start(f32[64,4,256]{2,1,0:T(4,128)S(1)} %get-tuple-element.75), channel_id=1, source_target_pairs={{4,0},{8,4},{12,8},{16,12},{20,16},{24,20},{28,24},{0,28},{5,1},{9... | collective-permute-start | bytes 786440 | tf_op jit(solution)/shard_map/ppermute | solution.py:22
  29.5 11.0 %collective-permute-start.5 = (f32[64,4,256]{2,1,0:T(4,128)S(1)}, f32[64,4,256]{2,1,0:T(4,128)S(1)}, u32[]{:S(2)}, u32[]{:S(2)}) collective-permute-start(f32[64,4,256]{2,1,0:T(4,128)S(1)} %get-tuple-element.76), channel_id=1, source_target_pairs={{0,4},{4,8},{8,12},{12,16},{16,20},{20,24},{24,28},{28,0},{1,5},{5... | collective-permute-start | bytes 786440 | tf_op jit(solution)/shard_map/ppermute | solution.py:21
  45.6 17.2 %collective-permute-start.10 = (f32[64,8,256]{2,1,0:T(8,128)S(1)}, f32[64,8,256]{2,1,0:T(8,128)S(1)}, u32[]{:S(2)}, u32[]{:S(2)}) collective-permute-start(f32[64,8,256]{2,1,0:T(8,128)S(1)} %fusion.33), channel_id=1, source_target_pairs={{1,0},{2,1},{3,2},{0,3},{5,4},{6,5},{7,6},{4,7},{9,8},{10,9},{11,1... | collective-permute-start | bytes 1572872 | tf_op jit(solution)/shard_map/ppermute | solution.py:22
  46.5 16.3 %collective-permute-start.11 = (f32[64,8,256]{2,1,0:T(8,128)S(1)}, f32[64,8,256]{2,1,0:T(8,128)S(1)}, u32[]{:S(2)}, u32[]{:S(2)}) collective-permute-start(f32[64,8,256]{2,1,0:T(8,128)S(1)} %fusion.33), channel_id=1, source_target_pairs={{0,1},{1,2},{2,3},{3,0},{4,5},{5,6},{6,7},{7,4},{8,9},{9,10},{10,1... | collective-permute-start | bytes 1572872 | tf_op jit(solution)/shard_map/ppermute | solution.py:21
  47.6 9.8 %collective-permute-start.8 = (f32[64,4,256]{2,1,0:T(4,128)S(1)}, f32[64,4,256]{2,1,0:T(4,128)S(1)}, u32[]{:S(2)}, u32[]{:S(2)}) collective-permute-start(f32[64,4,256]{2,1,0:T(4,128)S(1)} %get-tuple-element.41), channel_id=1, source_target_pairs={{4,0},{8,4},{12,8},{16,12},{20,16},{24,20},{28,24},{0,28},{5,1},{9... | collective-permute-start | bytes 786440 | tf_op jit(solution)/shard_map/ppermute | solution.py:22
  51.1 11.7 %collective-permute-start.9 = (f32[64,4,256]{2,1,0:T(4,128)S(1)}, f32[64,4,256]{2,1,0:T(4,128)S(1)}, u32[]{:S(2)}, u32[]{:S(2)}) collective-permute-start(f32[64,4,256]{2,1,0:T(4,128)S(1)} %get-tuple-element.42), channel_id=1, source_target_pairs={{0,4},{4,8},{8,12},{12,16},{16,20},{20,24},{24,28},{28,0},{1,5},{5... | collective-permute-start | bytes 786440 | tf_op jit(solution)/shard_map/ppermute | solution.py:21
where the time goes:
time: 176 us; the launch traced here: 175 us
  blocking collectives  80.5 us (46%)
  other arithmetic  35.1 us (20%)
  waiting for transfers between devices  28.6 us (16%)
  starting transfers between devices  16.2 us (9%)
  local copies, waits for them, and re-layouts  11.8 us (7%)
  matrix products  2.58 us (1%)
    psum x2, blocking collectives, orthonormal(): total_gram = lax.psum(local_gram, ('gx', 'gy'))  80.5 us
    ppermute x6, waiting for transfers between devices, padded(): after = lax.ppermute(first, axis, down)  18.6 us
    ppermute x6, starting transfers between devices, padded(): after = lax.ppermute(first, axis, down)  15.3 us
    another operation x6, other arithmetic, orthonormal(): lower_factor = jnp.linalg.cholesky(total_gram)  13 us
    another operation x4, other arithmetic, orthonormal(): lax.linalg.triangular_solve(lower_factor, matrix, left_side=True, lower=T...  11.1 us
    ppermute x6, waiting for transfers between devices, padded(): before = lax.ppermute(last, axis, up)  10.1 us
    sub x1, other arithmetic, on_device(): 2.0 * (hamiltonian(level_one, field_pot, depth_index) - CENTER * level_one)  3.83 us
    sub x1, other arithmetic, on_device(): 2.0 * (hamiltonian(second, field_pot, depth_index) - CENTER * second)  3.72 us
  transfers between devices with their start and end apart: 12, of which 6 were waited for; matrix products, arithmetic and copies ran while one was open for 4% of the time, Pallas kernels for 0%

commit v1 on v0

--- a/solution.py
+++ b/solution.py
@@ -1,6 +1,10 @@
+import functools
+
 import jax
 import jax.numpy as jnp
 from jax import lax
+from jax.experimental import pallas as pl
+from jax.experimental.pallas import tpu as pltpu
 from jax.sharding import PartitionSpec as P
 
 NZ = 64
@@ -88,9 +92,297 @@
     return final_pass.reshape(orbit_count, row_count, lane_count)
 
 
+MESH = pl.DeviceIdType.MESH
+EXACT = lax.Precision.HIGHEST
+LANES = 128
+
+
+def z_matrix():
+    row = lax.broadcasted_iota(jnp.int32, (LANES, LANES), 0)
+    col = lax.broadcasted_iota(jnp.int32, (LANES, LANES), 1)
+    same = (row // NZ) == (col // NZ)
+    gap = (row - col + 2 * NZ) % NZ
+    gap = jnp.minimum(gap, NZ - gap)
+    matrix = jnp.zeros((LANES, LANES), jnp.float32)
+    for distance in range(5):
+        if distance == 0:
+            value = (-1.5 * COEFS[0] - CENTER) / HALF_WIDTH
+        else:
+            value = -0.5 * COEFS[distance] / HALF_WIDTH
+        matrix = jnp.where(same & (gap == distance), value, matrix)
+    return matrix
+
+
+def dot_nn(a, b):
+    return lax.dot_general(a, b, (((1,), (0,)), ((), ())), precision=EXACT, preferred_element_type=jnp.float32)
+
+
+def dot_nt(a, b):
+    return lax.dot_general(a, b, (((1,), (1,)), ((), ())), precision=EXACT, preferred_element_type=jnp.float32)
+
+
+def inverse_factor(gram):
+    count = gram.shape[0]
+    tiles = count // 8
+    row_in = lax.broadcasted_iota(jnp.int32, (8, 2 * count), 0)
+    lane = lax.broadcasted_iota(jnp.int32, (8, 2 * count), 1)
+    blocks = []
+    for i in range(tiles):
+        eye = jnp.where(lane[:, :count] == row_in[:, :count] + 8 * i, 1.0, 0.0)
+        blocks.append(jnp.concatenate([gram[8 * i : 8 * i + 8], eye], axis=1))
+    for k in range(count - 1):
+        tile, sub = k // 8, k % 8
+        pivot_row = jnp.broadcast_to(blocks[tile][sub : sub + 1, :], (8, 2 * count))
+        pivot = jnp.broadcast_to(pivot_row[:, k : k + 1], (8, 2 * count))
+        scaled = pivot_row / pivot
+        for i in range(tile, tiles):
+            col = jnp.broadcast_to(blocks[i][:, k : k + 1], (8, 2 * count))
+            if i == tile:
+                col = jnp.where(row_in > sub, col, 0.0)
+            blocks[i] = blocks[i] - col * scaled
+    out = []
+    for i in range(tiles):
+        diagonal = jnp.sum(jnp.where(lane == row_in + 8 * i, blocks[i], 0.0), axis=1, keepdims=True)
+        out.append(blocks[i][:, count:] / jnp.sqrt(diagonal))
+    return jnp.concatenate(out, axis=0)
+
+
+def kernel(
+    nx, ny, psi_ref, pot_ref, out_ref,
+    send, field, pots, work, half, zpart, back, block, matrix, part, sum_a, sum_b,
+    psi_send, psi_recv, ret_send, ret_recv, pot_send, pot_recv, sum_send, sum_recv,
+):
+    devices = nx * ny
+    orbits = psi_ref.shape[0]
+    own = orbits // devices
+    planes = devices // 8
+    me = lax.axis_index("gx") * ny + lax.axis_index("gy")
+    my_plane, my_place = me // 8, me % 8
+
+    def device(target):
+        return (target // ny, target % ny)
+
+    def place_peer(step):
+        return my_plane * 8 + lax.rem(my_place + step, 8)
+
+    def plane_peer(step):
+        return lax.rem(my_plane + step, planes) * 8 + my_place
+
+    barrier = pltpu.get_barrier_semaphore()
+
+    def greet(i, _):
+        pl.semaphore_signal(barrier, inc=1, device_id=device(lax.rem(me + i, devices)), device_id_type=MESH)
+        return 0
+
+    lax.fori_loop(1, devices, greet, 0)
+
+    for h in range(2):
+        pots[my_place, my_plane, pl.ds(8 * h, 8), :] = pot_ref[:, h * LANES : (h + 1) * LANES] * (1.0 / HALF_WIDTH)
+    for m in range(orbits):
+        for h in range(2):
+            send[16 * m + 8 * h : 16 * m + 8 * h + 8, :] = psi_ref[m, :, h * LANES : (h + 1) * LANES]
+
+    pl.semaphore_wait(barrier, devices - 1)
+
+    def copy_out(src, dst, sems, target):
+        return pltpu.make_async_remote_copy(
+            src_ref=src, dst_ref=dst, send_sem=sems[0], recv_sem=sems[1],
+            device_id=device(target), device_id_type=MESH,
+        )
+
+    def drain(ref, sem):
+        pltpu.make_async_copy(ref, ref, sem).wait()
+
+    for step in range(1, planes):
+        here = pots.at[my_place, my_plane]
+        copy_out(here, here, (pot_send.at[0], pot_recv.at[0]), plane_peer(step)).start()
+
+    def send_psi(o):
+        def body(i, _):
+            target = lax.rem(me + i + devices // 2, devices)
+
+            @pl.when(target != me)
+            def _():
+                copy_out(
+                    send.at[pl.ds((target * own + o) * 16, 16)], field.at[o, me],
+                    (psi_send.at[o], psi_recv.at[o]), target,
+                ).start()
+            return 0
+
+        lax.fori_loop(0, devices, body, 0)
+        field[o, me] = send[pl.ds((me * own + o) * 16, 16), :]
+
+    send_psi(0)
+    drain(pots.at[0, pl.ds(0, planes - 1)], pot_recv.at[0])
+    drain(pots.at[0, pl.ds(0, planes - 1)], pot_send.at[0])
+    for step in range(1, 8):
+        here = pots.at[my_place]
+        copy_out(here, here, (pot_send.at[1], pot_recv.at[1]), place_peer(step)).start()
+    for o in range(1, own):
+        send_psi(o)
+
+    zmat = z_matrix()
+    tiles = 2 * ny
+    rows = 8 * nx
+    low = lax.broadcasted_iota(jnp.int32, (rows, LANES), 1) < NZ
+    weights = [-0.5 * c / HALF_WIDTH for c in COEFS]
+
+    def tile_of(ref, o, t):
+        return jnp.concatenate(
+            [ref[o, b * ny + t // 2, 8 * (t % 2) : 8 * (t % 2) + 8, :] for b in range(nx)], axis=0
+        )
+
+    def pot_tile(t):
+        parts = []
+        for b in range(nx):
+            d = b * ny + t // 2
+            parts.append(pots[d % 8, d // 8, 8 * (t % 2) : 8 * (t % 2) + 8, :])
+        return jnp.concatenate(parts, axis=0)
+
+    def apply(src, emit):
+        zpart[...] = dot_nn(work[src].reshape(tiles * rows, LANES), zmat).reshape(tiles, rows, LANES)
+        for t in range(tiles):
+            half[t] = pltpu.roll(work[src, t], NZ, 1)
+        for t in range(tiles):
+            v = work[src, t]
+            total = zpart[t] + pot_tile(t) * v
+            for d in range(1, 5):
+                total = total + weights[d] * (pltpu.roll(v, d, 0) + pltpu.roll(v, rows - d, 0))
+            total = total + weights[2] * (work[src, (t + 1) % tiles] + work[src, (t - 1) % tiles])
+            total = total + weights[4] * (work[src, (t + 2) % tiles] + work[src, (t - 2) % tiles])
+            s = [half[(t + k) % tiles] for k in range(-2, 3)]
+            total = total + weights[1] * (s[2] + jnp.where(low, s[1], s[3]))
+            total = total + weights[3] * jnp.where(low, s[3] + s[0], s[4] + s[1])
+            emit(t, total)
+
+    def send_back(o):
+        def body(i, _):
+            target = lax.rem(me + i + devices // 2, devices)
+
+            @pl.when(target != me)
+            def _():
+                copy_out(
+                    back.at[o, target], block.at[pl.ds((me * own + o) * 16, 16)],
+                    (ret_send.at[o], ret_recv), target,
+                ).start()
+            return 0
+
+        lax.fori_loop(0, devices, body, 0)
+        block[pl.ds((me * own + o) * 16, 16), :] = back[o, me]
+
+    for o in range(own):
+        drain(field.at[o, pl.ds(0, devices - 1)], psi_recv.at[o])
+        if o == 0:
+            drain(pots.at[pl.ds(0, 7)], pot_recv.at[1])
+        for t in range(tiles):
+            work[0, t] = tile_of(field, o, t)
+
+        def emit_one(t, value):
+            work[1, t] = value
+
+        def emit_two(t, value):
+            work[2, t] = 2.0 * value - work[0, t]
+
+        def emit_three(t, value):
+            value = 2.0 * value - work[1, t]
+            for b in range(nx):
+                back[o, b * ny + t // 2, 8 * (t % 2) : 8 * (t % 2) + 8, :] = value[8 * b : 8 * b + 8]
+
+        apply(0, emit_one)
+        apply(1, emit_two)
+        apply(2, emit_three)
+        send_back(o)
+
+    drain(pots.at[pl.ds(0, 7)], pot_send.at[1])
+    for o in range(own):
+        drain(field.at[o, pl.ds(0, devices - 1)], psi_send.at[o])
+        drain(back.at[o, pl.ds(0, devices - 1)], ret_send.at[o])
+    drain(block.at[pl.ds(0, (devices - 1) * own * 16)], ret_recv)
+
+    for j in range(16):
+        matrix[:, j * LANES : (j + 1) * LANES] = block[pl.ds(j, orbits, stride=16), :]
+
+    ncount = float(rows * tiles * LANES)
+    halfrows = orbits // 2
+
+    def total_gram(turn, local):
+        local = jnp.concatenate([local[:halfrows], local[halfrows:]], axis=1)
+        sum_a[turn, my_plane] = local
+        for step in range(1, planes):
+            here = sum_a.at[turn, my_plane]
+            copy_out(here, here, (sum_send.at[turn, 0], sum_recv.at[turn, 0]), plane_peer(step)).start()
+        drain(sum_a.at[turn, pl.ds(0, planes - 1)], sum_recv.at[turn, 0])
+        drain(sum_a.at[turn, pl.ds(0, planes - 1)], sum_send.at[turn, 0])
+        total = sum_a[turn, 0]
+        for i in range(1, planes):
+            total = total + sum_a[turn, i]
+        sum_b[turn, my_place] = total
+        for step in range(1, 8):
+            here = sum_b.at[turn, my_place]
+            copy_out(here, here, (sum_send.at[turn, 1], sum_recv.at[turn, 1]), place_peer(step)).start()
+        drain(sum_b.at[turn, pl.ds(0, 7)], sum_recv.at[turn, 1])
+        drain(sum_b.at[turn, pl.ds(0, 7)], sum_send.at[turn, 1])
+        total = sum_b[turn, 0]
+        for i in range(1, 8):
+            total = total + sum_b[turn, i]
+        total = total * (1.0 / ncount)
+        return jnp.concatenate([total[:, :orbits], total[:, orbits:]], axis=0)
+
+    for turn in range(2):
+        x = matrix[...]
+        gram = total_gram(turn, dot_nt(x, x))
+        matrix[...] = dot_nn(inverse_factor(gram), matrix[...])
+    for j in range(16):
+        block[pl.ds(j, orbits, stride=16), :] = matrix[:, j * LANES : (j + 1) * LANES]
+    for m in range(orbits):
+        for h in range(2):
+            out_ref[m, :, h * LANES : (h + 1) * LANES] = block[16 * m + 8 * h : 16 * m + 8 * h + 8, :]
+
+
+def transposed(nx, ny, psi, potential):
+    orbits = psi.shape[0]
+    devices = nx * ny
+    own = orbits // devices
+    f32 = jnp.float32
+    tiles, rows = 2 * ny, 8 * nx
+    dma = pltpu.SemaphoreType.DMA
+    return pl.pallas_call(
+        functools.partial(kernel, nx, ny),
+        out_shape=jax.ShapeDtypeStruct(psi.shape, f32),
+        in_specs=[pl.BlockSpec(memory_space=pltpu.VMEM)] * 2,
+        out_specs=pl.BlockSpec(memory_space=pltpu.VMEM),
+        scratch_shapes=[
+            pltpu.VMEM((orbits * 16, LANES), f32),
+            pltpu.VMEM((own, devices, 16, LANES), f32),
+            pltpu.VMEM((8, devices // 8, 16, LANES), f32),
+            pltpu.VMEM((3, tiles, rows, LANES), f32),
+            pltpu.VMEM((tiles, rows, LANES), f32),
+            pltpu.VMEM((tiles, rows, LANES), f32),
+            pltpu.VMEM((own, devices, 16, LANES), f32),
+            pltpu.VMEM((orbits * 16, LANES), f32),
+            pltpu.VMEM((orbits, 16 * LANES), f32),
+            pltpu.VMEM((8, LANES), f32),
+            pltpu.VMEM((2, devices // 8, orbits // 2, 2 * orbits), f32),
+            pltpu.VMEM((2, 8, orbits // 2, 2 * orbits), f32),
+            dma((own,)), dma((own,)), dma((own,)), dma,
+            dma((2,)), dma((2,)), dma((2, 2)), dma((2, 2)),
+        ],
+        compiler_params=pltpu.CompilerParams(
+            collective_id=0, has_side_effects=True, vmem_limit_bytes=48 * 1024 * 1024
+        ),
+    )(psi, potential)
+
+
 def solution(mesh):
     in_specs = (P(None, "gx", "gy"), P("gx", "gy"))
     out_specs = P(None, "gx", "gy")
-    return jax.shard_map(
-        on_device, mesh=mesh, in_specs=in_specs, out_specs=out_specs, check_vma=False
-    )
+    nx, ny = mesh.shape["gx"], mesh.shape["gy"]
+
+    def step(psi, potential):
+        orbits, rows, lanes = psi.shape
+        whole_orbits = orbits % (nx * ny) == 0 and (nx * ny) % 16 == 0
+        if whole_orbits and rows == 8 and lanes == 2 * LANES and orbits == 64 and ny >= 4:
+            return transposed(nx, ny, psi, potential)
+        return on_device(psi, potential)
+
+    return jax.shard_map(step, mesh=mesh, in_specs=in_specs, out_specs=out_specs, check_vma=False)

time: 176 us -> 71.9 us (0.41)
  blocking collectives: 80.5 us -> 0 us
  Pallas kernels: 0 us -> 69.1 us
  other arithmetic: 35.1 us -> 0 us
  waiting for transfers between devices: 28.6 us -> 0 us
  starting transfers between devices: 16.2 us -> 0 us
  local copies, waits for them, and re-layouts: 11.8 us -> 2.53 us
  matrix products: 2.58 us -> 0 us
    psum x2 -> x0, blocking collectives: 80.5 us -> none  [orthonormal(): total_gram = lax.psum(local_gram, ('gx', 'gy'))]
    pallas_call x0 -> x1, Pallas kernels: none -> 69.1 us  [transposed(): pl.pallas_call(functools.partial(kernel, nx, ny), out_shape=jax.ShapeDtyp...]
    ppermute x12 -> x0, waiting for transfers between devices: 28.6 us -> none  [the longest x6 18.6 us: padded(): after = lax.ppermute(first, axis, down)]
    another operation x10 -> x0, other arithmetic: 24.1 us -> none  [the longest x6 13 us: orthonormal(): lower_factor = jnp.linalg.cholesky(total_gram)]
    ppermute x12 -> x0, starting transfers between devices: 16.2 us -> none  [the longest x6 15.3 us: padded(): after = lax.ppermute(first, axis, down)]
    slice x51 -> x0, local copies, waits for them, and re-layouts: 9.58 us -> none  [the longest x16 2.68 us: along_third(): jnp.roll(field, distance, 2)]
    sub x2 -> x0, other arithmetic: 7.56 us -> none  [the longest x1 3.83 us: on_device(): 2.0 * (hamiltonian(level_one, field_pot, depth_index) - CENTER * level_one)]
    div x3 -> x0, other arithmetic: 3.36 us -> none  [the longest x1 3.34 us: on_device(): (hamiltonian(psi, field_pot, depth_index) - CENTER * psi) / HALF_WIDTH]
  transfers between devices with their start and end apart: 12 -> 0, of which waited for: 6 -> 0; matrix products, arithmetic and copies ran while one was open for 4% -> 0% of each run, Pallas kernels for 0% -> 0%
where the time goes in v1:
time: 71.9 us; the launch traced here: 71.7 us
  Pallas kernels  69.1 us (96%)
  local copies, waits for them, and re-layouts  2.53 us (4%)
    pallas_call x1, Pallas kernels, transposed(): pl.pallas_call(functools.partial(kernel, nx, ny), out_shape=jax.ShapeDtyp...  69.1 us
    unnamed x5, local copies, waits for them, and re-layouts  2.53 us

profile of v1, /device:TPU:0, one launch (start us, length us, event | category | flops | bytes accessed | tf_op | source)
XLA Modules:
  0.0 71.7 jit_solution(5037003620616174087)
XLA Ops:
  0.0 0.0 copy-start
  0.0 1.0 %copy-done = f32[64,8,256]{2,1,0:T(8,128)S(1)} copy-done((f32[64,8,256]{2,1,0:T(8,128)S(1)}, f32[64,8,256]{2,1,0:T(8,128)}, u32[]{:S(2)}) %copy-start) | copy-done | bytes 524312
  1.0 0.0 copy-start.1
  1.0 0.7 copy-done.1
  1.7 69.1 %shard_map.28 = f32[64,8,256]{2,1,0:T(8,128)S(1)} custom-call(f32[64,8,256]{2,1,0:T(8,128)S(1)} %copy-done, f32[8,256]{1,0:T(8,128)S(1)} %copy-done.1), custom_call_target="tpu_custom_call" | custom-call | tf_op jit(solution)/shard_map/pallas_call | solution.py:349
  70.9 0.8 %copy.4 = f32[64,8,256]{2,1,0:T(8,128)} copy(f32[64,8,256]{2,1,0:T(8,128)S(1)} %shard_map.28) | data formatting | bytes 1048576
Async XLA Ops:
  0.0 1.0 %copy-start = (f32[64,8,256]{2,1,0:T(8,128)S(1)}, f32[64,8,256]{2,1,0:T(8,128)}, u32[]{:S(2)}) copy-start(f32[64,8,256]{2,1,0:T(8,128)} %psi_ref.1) | copy-start | bytes 1572868
  1.0 0.7 copy-start.1

commit v2 on v1

--- a/solution.py
+++ b/solution.py
@@ -124,32 +124,60 @@
 def inverse_factor(gram):
     count = gram.shape[0]
     tiles = count // 8
-    row_in = lax.broadcasted_iota(jnp.int32, (8, 2 * count), 0)
-    lane = lax.broadcasted_iota(jnp.int32, (8, 2 * count), 1)
+    shape = (8, 2 * count)
+    row_in = lax.broadcasted_iota(jnp.int32, shape, 0)
+    lane = lax.broadcasted_iota(jnp.int32, shape, 1)
     blocks = []
     for i in range(tiles):
         eye = jnp.where(lane[:, :count] == row_in[:, :count] + 8 * i, 1.0, 0.0)
         blocks.append(jnp.concatenate([gram[8 * i : 8 * i + 8], eye], axis=1))
-    for k in range(count - 1):
-        tile, sub = k // 8, k % 8
-        pivot_row = jnp.broadcast_to(blocks[tile][sub : sub + 1, :], (8, 2 * count))
-        pivot = jnp.broadcast_to(pivot_row[:, k : k + 1], (8, 2 * count))
-        scaled = pivot_row / pivot
-        for i in range(tile, tiles):
-            col = jnp.broadcast_to(blocks[i][:, k : k + 1], (8, 2 * count))
-            if i == tile:
-                col = jnp.where(row_in > sub, col, 0.0)
-            blocks[i] = blocks[i] - col * scaled
+
+    def row_of(array, j):
+        return jnp.broadcast_to(array[j : j + 1, :], shape)
+
     out = []
-    for i in range(tiles):
-        diagonal = jnp.sum(jnp.where(lane == row_in + 8 * i, blocks[i], 0.0), axis=1, keepdims=True)
-        out.append(blocks[i][:, count:] / jnp.sqrt(diagonal))
+    for t in range(tiles):
+        cols = [[jnp.broadcast_to(blocks[i][:, 8 * t + j : 8 * t + j + 1], shape) for j in range(8)] for i in range(t, tiles)]
+        diag = [[row_of(cols[0][j], a) if a >= j else None for j in range(8)] for a in range(8)]
+        inverse, pivots = [], []
+        factor = [[None] * 8 for _ in range(8)]
+        for j in range(8):
+            pivots.append(diag[j][j])
+            inverse.append(1.0 / diag[j][j])
+            for a in range(j + 1, 8):
+                factor[a][j] = diag[a][j] * inverse[j]
+            for a in range(j + 1, 8):
+                for b in range(j + 1, a + 1):
+                    diag[a][b] = diag[a][b] - factor[a][j] * diag[b][j]
+        current = blocks[t]
+        finished = []
+        for j in range(8):
+            finished.append(row_of(current, j))
+            if j < 7:
+                below = jnp.zeros(shape, jnp.float32)
+                for a in range(j + 1, 8):
+                    below = jnp.where(row_in == a, factor[a][j], below)
+                current = current - below * finished[j]
+        blocks[t] = current
+        for i in range(t + 1, tiles):
+            col = cols[i - t]
+            total = blocks[i]
+            for j in range(8):
+                scaled = col[j] * inverse[j]
+                total = total - scaled * finished[j]
+                for b in range(j + 1, 8):
+                    col[b] = col[b] - scaled * diag[b][j]
+            blocks[i] = total
+        pivot = pivots[0]
+        for j in range(1, 8):
+            pivot = jnp.where(row_in == j, pivots[j], pivot)
+        out.append((current / jnp.sqrt(pivot))[:, count:])
     return jnp.concatenate(out, axis=0)
 
 
 def kernel(
     nx, ny, psi_ref, pot_ref, out_ref,
-    send, field, pots, work, half, zpart, back, block, matrix, part, sum_a, sum_b,
+    send, field, pots, work, half, zpart, back, block, matrix, pot_in, sum_a, sum_b, load_sem,
     psi_send, psi_recv, ret_send, ret_recv, pot_send, pot_recv, sum_send, sum_recv,
 ):
     devices = nx * ny
@@ -168,6 +196,18 @@
     def plane_peer(step):
         return lax.rem(my_plane + step, planes) * 8 + my_place
 
+    loads = []
+    for h in range(2):
+        half_lanes = pl.ds(h * LANES, LANES)
+        loads.append(pltpu.make_async_copy(
+            psi_ref.at[:, :, half_lanes], send.at[:, pl.ds(8 * h, 8), :], load_sem.at[h]))
+    for h in range(2):
+        half_lanes = pl.ds(h * LANES, LANES)
+        loads.append(pltpu.make_async_copy(
+            pot_ref.at[:, half_lanes], pot_in.at[pl.ds(8 * h, 8), :], load_sem.at[2 + h]))
+    for c in loads:
+        c.start()
+
     barrier = pltpu.get_barrier_semaphore()
 
     def greet(i, _):
@@ -176,12 +216,9 @@
 
     lax.fori_loop(1, devices, greet, 0)
 
-    for h in range(2):
-        pots[my_place, my_plane, pl.ds(8 * h, 8), :] = pot_ref[:, h * LANES : (h + 1) * LANES] * (1.0 / HALF_WIDTH)
-    for m in range(orbits):
-        for h in range(2):
-            send[16 * m + 8 * h : 16 * m + 8 * h + 8, :] = psi_ref[m, :, h * LANES : (h + 1) * LANES]
-
+    for c in loads[2:]:
+        c.wait()
+    pots[my_place, my_plane] = pot_in[...] * (1.0 / HALF_WIDTH)
     pl.semaphore_wait(barrier, devices - 1)
 
     def copy_out(src, dst, sems, target):
@@ -204,14 +241,16 @@
             @pl.when(target != me)
             def _():
                 copy_out(
-                    send.at[pl.ds((target * own + o) * 16, 16)], field.at[o, me],
+                    send.at[target * own + o], field.at[o, me],
                     (psi_send.at[o], psi_recv.at[o]), target,
                 ).start()
             return 0
 
         lax.fori_loop(0, devices, body, 0)
-        field[o, me] = send[pl.ds((me * own + o) * 16, 16), :]
-
+        field[o, me] = send[me * own + o]
+
+    for c in loads[:2]:
+        c.wait()
     send_psi(0)
     drain(pots.at[0, pl.ds(0, planes - 1)], pot_recv.at[0])
     drain(pots.at[0, pl.ds(0, planes - 1)], pot_send.at[0])
@@ -349,10 +388,10 @@
     return pl.pallas_call(
         functools.partial(kernel, nx, ny),
         out_shape=jax.ShapeDtypeStruct(psi.shape, f32),
-        in_specs=[pl.BlockSpec(memory_space=pltpu.VMEM)] * 2,
+        in_specs=[pl.BlockSpec(memory_space=pl.ANY)] * 2,
         out_specs=pl.BlockSpec(memory_space=pltpu.VMEM),
         scratch_shapes=[
-            pltpu.VMEM((orbits * 16, LANES), f32),
+            pltpu.VMEM((orbits, 16, LANES), f32),
             pltpu.VMEM((own, devices, 16, LANES), f32),
             pltpu.VMEM((8, devices // 8, 16, LANES), f32),
             pltpu.VMEM((3, tiles, rows, LANES), f32),
@@ -361,10 +400,10 @@
             pltpu.VMEM((own, devices, 16, LANES), f32),
             pltpu.VMEM((orbits * 16, LANES), f32),
             pltpu.VMEM((orbits, 16 * LANES), f32),
-            pltpu.VMEM((8, LANES), f32),
+            pltpu.VMEM((16, LANES), f32),
             pltpu.VMEM((2, devices // 8, orbits // 2, 2 * orbits), f32),
             pltpu.VMEM((2, 8, orbits // 2, 2 * orbits), f32),
-            dma((own,)), dma((own,)), dma((own,)), dma,
+            dma((4,)), dma((own,)), dma((own,)), dma((own,)), dma,
             dma((2,)), dma((2,)), dma((2, 2)), dma((2, 2)),
         ],
         compiler_params=pltpu.CompilerParams(

time: 71.9 us -> 59.2 us (0.82)
  Pallas kernels: 69.1 us -> 56.5 us
    pallas_call x1, Pallas kernels: 69.1 us -> 56.5 us  [transposed(): pl.pallas_call(functools.partial(kernel, nx, ny), out_shape=jax.ShapeDtyp...]
where the time goes in v2:
time: 59.2 us; the launch traced here: 59 us
  Pallas kernels  56.5 us (95%)
  local copies, waits for them, and re-layouts  2.53 us (4%)
    pallas_call x1, Pallas kernels, transposed(): pl.pallas_call(functools.partial(kernel, nx, ny), out_shape=jax.ShapeDtyp...  56.5 us
    unnamed x5, local copies, waits for them, and re-layouts  2.53 us

profile of v2, /device:TPU:0, one launch (start us, length us, event | category | flops | bytes accessed | tf_op | source)
XLA Modules:
  0.0 59.0 jit_solution(11146014272604401197)
XLA Ops:
  0.0 0.0 copy-start
  0.0 1.0 %copy-done = f32[64,8,256]{2,1,0:T(8,128)S(1)} copy-done((f32[64,8,256]{2,1,0:T(8,128)S(1)}, f32[64,8,256]{2,1,0:T(8,128)}, u32[]{:S(2)}) %copy-start) | copy-done | bytes 524312
  1.0 0.0 copy-start.1
  1.0 0.7 %copy-done.1 = f32[8,256]{1,0:T(8,128)S(1)} copy-done((f32[8,256]{1,0:T(8,128)S(1)}, f32[8,256]{1,0:T(8,128)}, u32[]{:S(2)}) %copy-start.1) | copy-done | bytes 8216
  1.7 56.5 %shard_map.28 = f32[64,8,256]{2,1,0:T(8,128)S(1)} custom-call(f32[64,8,256]{2,1,0:T(8,128)S(1)} %copy-done, f32[8,256]{1,0:T(8,128)S(1)} %copy-done.1), custom_call_target="tpu_custom_call" | custom-call | tf_op jit(solution)/shard_map/pallas_call | solution.py:388
  58.2 0.8 %copy.4 = f32[64,8,256]{2,1,0:T(8,128)} copy(f32[64,8,256]{2,1,0:T(8,128)S(1)} %shard_map.28) | data formatting | bytes 1048576
Async XLA Ops:
  0.0 1.0 %copy-start = (f32[64,8,256]{2,1,0:T(8,128)S(1)}, f32[64,8,256]{2,1,0:T(8,128)}, u32[]{:S(2)}) copy-start(f32[64,8,256]{2,1,0:T(8,128)} %psi_ref.1) | copy-start | bytes 1572868
  1.0 0.7 %copy-start.1 = (f32[8,256]{1,0:T(8,128)S(1)}, f32[8,256]{1,0:T(8,128)}, u32[]{:S(2)}) copy-start(f32[8,256]{1,0:T(8,128)} %pot_ref.1) | copy-start | bytes 24580

commit v3 on v2

--- a/solution.py
+++ b/solution.py
@@ -1,4 +1,5 @@
 import functools
+import math
 
 import jax
 import jax.numpy as jnp
@@ -143,7 +144,9 @@
         factor = [[None] * 8 for _ in range(8)]
         for j in range(8):
             pivots.append(diag[j][j])
-            inverse.append(1.0 / diag[j][j])
+            guess = pl.reciprocal(diag[j][j], approx=True)
+            guess = guess * (2.0 - diag[j][j] * guess)
+            inverse.append(guess * (2.0 - diag[j][j] * guess))
             for a in range(j + 1, 8):
                 factor[a][j] = diag[a][j] * inverse[j]
             for a in range(j + 1, 8):
@@ -234,19 +237,18 @@
         here = pots.at[my_place, my_plane]
         copy_out(here, here, (pot_send.at[0], pot_recv.at[0]), plane_peer(step)).start()
 
+    stride = next(n for n in (13, 11, 7, 5, 3, 1) if math.gcd(n, devices) == 1)
+
     def send_psi(o):
         def body(i, _):
-            target = lax.rem(me + i + devices // 2, devices)
-
-            @pl.when(target != me)
-            def _():
-                copy_out(
-                    send.at[target * own + o], field.at[o, me],
-                    (psi_send.at[o], psi_recv.at[o]), target,
-                ).start()
+            target = lax.rem(me + i * stride, devices)
+            copy_out(
+                send.at[target * own + o], field.at[o, me],
+                (psi_send.at[o], psi_recv.at[o]), target,
+            ).start()
             return 0
 
-        lax.fori_loop(0, devices, body, 0)
+        lax.fori_loop(1, devices, body, 0)
         field[o, me] = send[me * own + o]
 
     for c in loads[:2]:
@@ -296,17 +298,14 @@
 
     def send_back(o):
         def body(i, _):
-            target = lax.rem(me + i + devices // 2, devices)
-
-            @pl.when(target != me)
-            def _():
-                copy_out(
-                    back.at[o, target], block.at[pl.ds((me * own + o) * 16, 16)],
-                    (ret_send.at[o], ret_recv), target,
-                ).start()
+            target = lax.rem(me + i * stride, devices)
+            copy_out(
+                back.at[o, target], block.at[pl.ds((me * own + o) * 16, 16)],
+                (ret_send.at[o], ret_recv), target,
+            ).start()
             return 0
 
-        lax.fori_loop(0, devices, body, 0)
+        lax.fori_loop(1, devices, body, 0)
         block[pl.ds((me * own + o) * 16, 16), :] = back[o, me]
 
     for o in range(own):
@@ -407,7 +406,7 @@
             dma((2,)), dma((2,)), dma((2, 2)), dma((2, 2)),
         ],
         compiler_params=pltpu.CompilerParams(
-            collective_id=0, has_side_effects=True, vmem_limit_bytes=48 * 1024 * 1024
+            collective_id=0, has_side_effects=True
         ),
     )(psi, potential)
 

time: 59.2 us -> 58.8 us (level)
  local copies, waits for them, and re-layouts: 2.53 us -> 1.87 us
    unnamed x5 -> x1, local copies, waits for them, and re-layouts: 2.53 us -> 1.87 us
where the time goes in v3:
time: 58.8 us; the launch traced here: 58.6 us
  Pallas kernels  56.8 us (97%)
  local copies, waits for them, and re-layouts  1.87 us (3%)
    pallas_call x1, Pallas kernels, transposed(): pl.pallas_call(functools.partial(kernel, nx, ny), out_shape=jax.ShapeDtyp...  56.8 us
    unnamed x1, local copies, waits for them, and re-layouts  1.87 us

profile of v3, /device:TPU:0, one launch (start us, length us, event | category | flops | bytes accessed | tf_op | source)
XLA Modules:
  0.0 58.6 jit_solution(9700714484452385907)
XLA Ops:
  0.0 56.8 %shard_map.28 = f32[64,8,256]{2,1,0:T(8,128)} custom-call(f32[64,8,256]{2,1,0:T(8,128)} %psi_ref.1, f32[8,256]{1,0:T(8,128)} %pot_ref.1), custom_call_target="tpu_custom_call" | custom-call | tf_op jit(solution)/shard_map/pallas_call | solution.py:387
  56.8 1.9 %copy.4 = f32[64,8,256]{2,1,0:T(8,128)} copy(f32[64,8,256]{2,1,0:T(8,128)} %shard_map.28) | data formatting | bytes 1048576

commit v4 on v3

--- a/solution.py
+++ b/solution.py
@@ -123,15 +123,15 @@
 
 
 def inverse_factor(gram):
-    count = gram.shape[0]
-    tiles = count // 8
+    tiles = len(gram)
+    count = 8 * tiles
     shape = (8, 2 * count)
     row_in = lax.broadcasted_iota(jnp.int32, shape, 0)
     lane = lax.broadcasted_iota(jnp.int32, shape, 1)
     blocks = []
     for i in range(tiles):
-        eye = jnp.where(lane[:, :count] == row_in[:, :count] + 8 * i, 1.0, 0.0)
-        blocks.append(jnp.concatenate([gram[8 * i : 8 * i + 8], eye], axis=1))
+        eye = jnp.where(lane == row_in + 8 * i + count, 1.0, 0.0)
+        blocks.append(jnp.where(lane < count, gram[i], eye))
 
     def row_of(array, j):
         return jnp.broadcast_to(array[j : j + 1, :], shape)
@@ -179,8 +179,8 @@
 
 
 def kernel(
-    nx, ny, psi_ref, pot_ref, out_ref,
-    send, field, pots, work, half, zpart, back, block, matrix, pot_in, sum_a, sum_b, load_sem,
+    nx, ny, psi_ref, pot_ref, first_ref, factor_ref,
+    send, field, pots, work, half, zpart, back, block, matrix, pot_in, sum_out, sum_a, sum_b, sum_c, load_sem,
     psi_send, psi_recv, ret_send, ret_recv, pot_send, pot_recv, sum_send, sum_recv,
 ):
     devices = nx * ny
@@ -331,50 +331,70 @@
         apply(2, emit_three)
         send_back(o)
 
+    drain(block.at[pl.ds(0, (devices - 1) * own * 16)], ret_recv)
+
+    for j in range(16):
+        matrix[:, j * LANES : (j + 1) * LANES] = block[pl.ds(j, orbits, stride=16), :]
+
+    ncount = float(rows * tiles * LANES)
+    pieces = orbits // 8
+
+    def total_gram(turn, local):
+        local = jnp.concatenate([local, jnp.zeros_like(local)], axis=1)
+        for p in range(pieces):
+            sum_out[turn, p] = local[8 * p : 8 * p + 8]
+        for step in range(1, 8):
+            peer = lax.rem(my_place + step, 8)
+            copy_out(
+                sum_out.at[turn, peer], sum_a.at[turn, my_place],
+                (sum_send.at[turn, 0], sum_recv.at[turn, 0]), my_plane * 8 + peer,
+            ).start()
+        sum_a[turn, my_place] = sum_out[turn, my_place]
+        drain(sum_a.at[turn, pl.ds(0, 7)], sum_recv.at[turn, 0])
+        total = sum_a[turn, 0]
+        for i in range(1, 8):
+            total = total + sum_a[turn, i]
+        sum_b[turn, my_plane] = total
+        for step in range(1, planes):
+            here = sum_b.at[turn, my_plane]
+            copy_out(here, here, (sum_send.at[turn, 1], sum_recv.at[turn, 1]), plane_peer(step)).start()
+        drain(sum_b.at[turn, pl.ds(0, planes - 1)], sum_recv.at[turn, 1])
+        total = sum_b[turn, 0]
+        for i in range(1, planes):
+            total = total + sum_b[turn, i]
+        sum_c[turn, my_place] = total * (1.0 / ncount)
+        for step in range(1, 8):
+            here = sum_c.at[turn, my_place]
+            copy_out(here, here, (sum_send.at[turn, 2], sum_recv.at[turn, 2]), place_peer(step)).start()
+        drain(sum_c.at[turn, pl.ds(0, 7)], sum_recv.at[turn, 2])
+        return [sum_c[turn, p] for p in range(pieces)]
+
+    x = matrix[...]
+    gram = total_gram(0, dot_nt(x, x))
+    matrix[...] = dot_nn(inverse_factor(gram), matrix[...])
+    store = pltpu.make_async_copy(matrix, first_ref, load_sem.at[0])
+    store.start()
+    x = matrix[...]
+    gram = total_gram(1, dot_nt(x, x))
+    factor_ref[...] = inverse_factor(gram)
+
+    store.wait()
     drain(pots.at[pl.ds(0, 7)], pot_send.at[1])
     for o in range(own):
         drain(field.at[o, pl.ds(0, devices - 1)], psi_send.at[o])
         drain(back.at[o, pl.ds(0, devices - 1)], ret_send.at[o])
-    drain(block.at[pl.ds(0, (devices - 1) * own * 16)], ret_recv)
-
-    for j in range(16):
-        matrix[:, j * LANES : (j + 1) * LANES] = block[pl.ds(j, orbits, stride=16), :]
-
-    ncount = float(rows * tiles * LANES)
-    halfrows = orbits // 2
-
-    def total_gram(turn, local):
-        local = jnp.concatenate([local[:halfrows], local[halfrows:]], axis=1)
-        sum_a[turn, my_plane] = local
-        for step in range(1, planes):
-            here = sum_a.at[turn, my_plane]
-            copy_out(here, here, (sum_send.at[turn, 0], sum_recv.at[turn, 0]), plane_peer(step)).start()
-        drain(sum_a.at[turn, pl.ds(0, planes - 1)], sum_recv.at[turn, 0])
-        drain(sum_a.at[turn, pl.ds(0, planes - 1)], sum_send.at[turn, 0])
-        total = sum_a[turn, 0]
-        for i in range(1, planes):
-            total = total + sum_a[turn, i]
-        sum_b[turn, my_place] = total
-        for step in range(1, 8):
-            here = sum_b.at[turn, my_place]
-            copy_out(here, here, (sum_send.at[turn, 1], sum_recv.at[turn, 1]), place_peer(step)).start()
-        drain(sum_b.at[turn, pl.ds(0, 7)], sum_recv.at[turn, 1])
-        drain(sum_b.at[turn, pl.ds(0, 7)], sum_send.at[turn, 1])
-        total = sum_b[turn, 0]
-        for i in range(1, 8):
-            total = total + sum_b[turn, i]
-        total = total * (1.0 / ncount)
-        return jnp.concatenate([total[:, :orbits], total[:, orbits:]], axis=0)
-
     for turn in range(2):
-        x = matrix[...]
-        gram = total_gram(turn, dot_nt(x, x))
-        matrix[...] = dot_nn(inverse_factor(gram), matrix[...])
-    for j in range(16):
-        block[pl.ds(j, orbits, stride=16), :] = matrix[:, j * LANES : (j + 1) * LANES]
-    for m in range(orbits):
-        for h in range(2):
-            out_ref[m, :, h * LANES : (h + 1) * LANES] = block[16 * m + 8 * h : 16 * m + 8 * h + 8, :]
+        drain(sum_a.at[turn, pl.ds(0, 7)], sum_send.at[turn, 0])
+        drain(sum_b.at[turn, pl.ds(0, planes - 1)], sum_send.at[turn, 1])
+        drain(sum_c.at[turn, pl.ds(0, 7)], sum_send.at[turn, 2])
+
+
+def finish(factor_ref, first_ref, out_ref):
+    orbits = factor_ref.shape[0]
+    value = dot_nn(factor_ref[...], first_ref[...])
+    flat = out_ref.reshape(orbits * 8, LANES)
+    for r in range(8):
+        flat[pl.ds(r, orbits, stride=8), :] = value[:, r * LANES : (r + 1) * LANES]
 
 
 def transposed(nx, ny, psi, potential):
@@ -384,11 +404,14 @@
     f32 = jnp.float32
     tiles, rows = 2 * ny, 8 * nx
     dma = pltpu.SemaphoreType.DMA
-    return pl.pallas_call(
+    first, factor = pl.pallas_call(
         functools.partial(kernel, nx, ny),
-        out_shape=jax.ShapeDtypeStruct(psi.shape, f32),
+        out_shape=(
+            jax.ShapeDtypeStruct((orbits, 16 * LANES), f32),
+            jax.ShapeDtypeStruct((orbits, orbits), f32),
+        ),
         in_specs=[pl.BlockSpec(memory_space=pl.ANY)] * 2,
-        out_specs=pl.BlockSpec(memory_space=pltpu.VMEM),
+        out_specs=(pl.BlockSpec(memory_space=pl.ANY), pl.BlockSpec(memory_space=pltpu.VMEM)),
         scratch_shapes=[
             pltpu.VMEM((orbits, 16, LANES), f32),
             pltpu.VMEM((own, devices, 16, LANES), f32),
@@ -400,15 +423,27 @@
             pltpu.VMEM((orbits * 16, LANES), f32),
             pltpu.VMEM((orbits, 16 * LANES), f32),
             pltpu.VMEM((16, LANES), f32),
-            pltpu.VMEM((2, devices // 8, orbits // 2, 2 * orbits), f32),
-            pltpu.VMEM((2, 8, orbits // 2, 2 * orbits), f32),
+            pltpu.VMEM((2, 8, 8, LANES), f32),
+            pltpu.VMEM((2, 8, 8, LANES), f32),
+            pltpu.VMEM((2, devices // 8, 8, LANES), f32),
+            pltpu.VMEM((2, 8, 8, LANES), f32),
             dma((4,)), dma((own,)), dma((own,)), dma((own,)), dma,
-            dma((2,)), dma((2,)), dma((2, 2)), dma((2, 2)),
+            dma((2,)), dma((2,)), dma((2, 3)), dma((2, 3)),
         ],
         compiler_params=pltpu.CompilerParams(
             collective_id=0, has_side_effects=True
         ),
     )(psi, potential)
+    return pl.pallas_call(
+        finish,
+        grid=(2,),
+        out_shape=jax.ShapeDtypeStruct(psi.shape, f32),
+        in_specs=[
+            pl.BlockSpec((orbits, orbits), lambda h: (0, 0)),
+            pl.BlockSpec((orbits, 8 * LANES), lambda h: (0, h)),
+        ],
+        out_specs=pl.BlockSpec((orbits, 8, LANES), lambda h: (0, 0, h)),
+    )(factor, first)
 
 
 def solution(mesh):

time: 58.8 us -> 62.9 us (1.070)
  Pallas kernels: 56.8 us -> 62.8 us
  local copies, waits for them, and re-layouts: 1.87 us -> 0 us
    pallas_call x1 -> x2, Pallas kernels: 56.8 us -> 62.8 us  [the longest x1 60.3 us: transposed(): pl.pallas_call(functools.partial(kernel, nx, ny), out_shape=(jax.ShapeDty...]
    unnamed x1 -> x0, local copies, waits for them, and re-layouts: 1.87 us -> none
where the time goes in v4:
time: 62.9 us; the launch traced here: 62.8 us
  Pallas kernels  62.8 us (100%)
    pallas_call x1, Pallas kernels, transposed(): pl.pallas_call(functools.partial(kernel, nx, ny), out_shape=(jax.ShapeDty...  60.3 us
    pallas_call x1, Pallas kernels, transposed(): pl.pallas_call(finish, grid=(2,), out_shape=jax.ShapeDtypeStruct(psi.shap...  2.43 us

profile of v4, /device:TPU:0, one launch (start us, length us, event | category | flops | bytes accessed | tf_op | source)
XLA Modules:
  0.0 62.8 jit_solution(2786995335476326044)
XLA Ops:
  0.0 60.3 %shard_map.28 = (f32[64,2048]{1,0:T(8,128)}, f32[64,64]{1,0:T(8,128)}) custom-call(f32[64,8,256]{2,1,0:T(8,128)} %psi_ref.1, f32[8,256]{1,0:T(8,128)} %pot_ref.1), custom_call_target="tpu_custom_call" | custom-call | tf_op jit(solution)/shard_map/pallas_call | solution.py:407
  60.3 2.4 %shard_map.29 = f32[64,8,256]{2,1,0:T(8,128)} custom-call(f32[64,64]{1,0:T(8,128)} %get-tuple-element.7.factor_ref, f32[64,2048]{1,0:T(8,128)} %get-tuple-element.8.first_ref), custom_call_target="tpu_custom_call" | custom-call | tf_op jit(solution)/shard_map/pallas_call | solution.py:437

commit v5 on v4

--- a/solution.py
+++ b/solution.py
@@ -178,9 +178,64 @@
     return jnp.concatenate(out, axis=0)
 
 
+def two_sum(a, b):
+    total = a + b
+    part = total - a
+    return total, (a - (total - part)) + (b - part)
+
+
+def pair_add(first, second):
+    total, rest = two_sum(first[0], second[0])
+    return total, rest + (first[1] + second[1])
+
+
+def settle(pair):
+    total = pair[0] + pair[1]
+    return total, pair[1] - (total - pair[0])
+
+
+def slices(pair, count):
+    value, rest = pair
+    size = jnp.max(jnp.abs(value), axis=1, keepdims=True) * 2.0**17
+    out = []
+    for p in range(count):
+        if p == 3 and rest is not None:
+            value = value + rest
+        unit = size * 2.0 ** (-7 * p)
+        term = (value + unit) - unit
+        out.append(term.astype(jnp.bfloat16))
+        value = value - term
+    return out
+
+
+def exact_products(left, right, depth):
+    rows, total = left[0].shape
+    stacked = jnp.concatenate(left, axis=0)
+    pair = None
+    for start in range(0, total, depth):
+        orders = {}
+        for q in range(0, len(right), 2):
+            other = jnp.concatenate(right[q : q + 2], axis=0)
+            product = lax.dot_general(
+                stacked[:, start : start + depth], other[:, start : start + depth],
+                (((1,), (1,)), ((), ())), preferred_element_type=jnp.float32,
+            )
+            for p in range(len(left)):
+                block = product[rows * p : rows * p + rows]
+                orders[p + q] = orders[p + q] + block if p + q in orders else block
+        for order in sorted(orders):
+            if pair is None:
+                pair = orders[order], jnp.zeros_like(orders[order])
+            else:
+                value, rest = two_sum(pair[0], orders[order])
+                pair = value, pair[1] + rest
+    turned = pltpu.roll(pair[0], rows, 1), pltpu.roll(pair[1], rows, 1)
+    return settle(pair_add(pair, turned))
+
+
 def kernel(
     nx, ny, psi_ref, pot_ref, first_ref, factor_ref,
-    send, field, pots, work, half, zpart, back, block, matrix, pot_in, sum_out, sum_a, sum_b, sum_c, load_sem,
+    send, field, pots, work, half, zpart, back, block, matrix, pot_in, sum_a, sum_b, load_sem,
     psi_send, psi_recv, ret_send, ret_recv, pot_send, pot_recv, sum_send, sum_recv,
 ):
     devices = nx * ny
@@ -337,56 +392,56 @@
         matrix[:, j * LANES : (j + 1) * LANES] = block[pl.ds(j, orbits, stride=16), :]
 
     ncount = float(rows * tiles * LANES)
-    pieces = orbits // 8
-
-    def total_gram(turn, local):
-        local = jnp.concatenate([local, jnp.zeros_like(local)], axis=1)
-        for p in range(pieces):
-            sum_out[turn, p] = local[8 * p : 8 * p + 8]
+    upper = orbits // 2
+
+    def total_gram(local):
+        low_lane = lax.broadcasted_iota(jnp.int32, (upper, 2 * orbits), 1) < orbits
+        for i in range(2):
+            sum_a[my_plane, i] = jnp.where(low_lane, local[i][:upper], local[i][upper:])
+        for step in range(1, planes):
+            here = sum_a.at[my_plane]
+            copy_out(here, here, (sum_send.at[0], sum_recv.at[0]), plane_peer(step)).start()
+        drain(sum_a.at[pl.ds(0, planes - 1)], sum_recv.at[0])
+        total = sum_a[0, 0], sum_a[0, 1]
+        for i in range(1, planes):
+            total = pair_add(total, (sum_a[i, 0], sum_a[i, 1]))
+        for i in range(2):
+            sum_b[my_place, i] = total[i]
         for step in range(1, 8):
-            peer = lax.rem(my_place + step, 8)
-            copy_out(
-                sum_out.at[turn, peer], sum_a.at[turn, my_place],
-                (sum_send.at[turn, 0], sum_recv.at[turn, 0]), my_plane * 8 + peer,
-            ).start()
-        sum_a[turn, my_place] = sum_out[turn, my_place]
-        drain(sum_a.at[turn, pl.ds(0, 7)], sum_recv.at[turn, 0])
-        total = sum_a[turn, 0]
+            here = sum_b.at[my_place]
+            copy_out(here, here, (sum_send.at[1], sum_recv.at[1]), place_peer(step)).start()
+        drain(sum_b.at[pl.ds(0, 7)], sum_recv.at[1])
+        total = sum_b[0, 0], sum_b[0, 1]
         for i in range(1, 8):
-            total = total + sum_a[turn, i]
-        sum_b[turn, my_plane] = total
-        for step in range(1, planes):
-            here = sum_b.at[turn, my_plane]
-            copy_out(here, here, (sum_send.at[turn, 1], sum_recv.at[turn, 1]), plane_peer(step)).start()
-        drain(sum_b.at[turn, pl.ds(0, planes - 1)], sum_recv.at[turn, 1])
-        total = sum_b[turn, 0]
-        for i in range(1, planes):
-            total = total + sum_b[turn, i]
-        sum_c[turn, my_place] = total * (1.0 / ncount)
-        for step in range(1, 8):
-            here = sum_c.at[turn, my_place]
-            copy_out(here, here, (sum_send.at[turn, 2], sum_recv.at[turn, 2]), place_peer(step)).start()
-        drain(sum_c.at[turn, pl.ds(0, 7)], sum_recv.at[turn, 2])
-        return [sum_c[turn, p] for p in range(pieces)]
-
-    x = matrix[...]
-    gram = total_gram(0, dot_nt(x, x))
-    matrix[...] = dot_nn(inverse_factor(gram), matrix[...])
+            total = pair_add(total, (sum_b[i, 0], sum_b[i, 1]))
+        total = settle(total)
+        return [
+            jnp.concatenate([part, pltpu.roll(part, orbits, 1)], axis=0) * (1.0 / ncount) for part in total
+        ]
+
+    def tiles_of(array):
+        return [array[8 * i : 8 * i + 8] for i in range(orbits // 8)]
+
+    parts = slices((matrix[...], None), 4)
+    gram = total_gram(exact_products(parts, parts, 8 * LANES))
+    inverse = inverse_factor(tiles_of(gram[0]))
+    matrix[...] = dot_nn(inverse, matrix[...])
     store = pltpu.make_async_copy(matrix, first_ref, load_sem.at[0])
     store.start()
-    x = matrix[...]
-    gram = total_gram(1, dot_nt(x, x))
-    factor_ref[...] = inverse_factor(gram)
+    inverse_parts = slices((inverse, None), 6)
+    gram_parts = slices((gram[0][:, :orbits], gram[1][:, :orbits]), 6)
+    half_way = exact_products(inverse_parts, gram_parts, orbits)
+    half_parts = slices((half_way[0][:, :orbits], half_way[1][:, :orbits]), 6)
+    second = exact_products(half_parts, inverse_parts, orbits)
+    factor_ref[...] = inverse_factor(tiles_of(second[0]))
 
     store.wait()
     drain(pots.at[pl.ds(0, 7)], pot_send.at[1])
     for o in range(own):
         drain(field.at[o, pl.ds(0, devices - 1)], psi_send.at[o])
         drain(back.at[o, pl.ds(0, devices - 1)], ret_send.at[o])
-    for turn in range(2):
-        drain(sum_a.at[turn, pl.ds(0, 7)], sum_send.at[turn, 0])
-        drain(sum_b.at[turn, pl.ds(0, planes - 1)], sum_send.at[turn, 1])
-        drain(sum_c.at[turn, pl.ds(0, 7)], sum_send.at[turn, 2])
+    drain(sum_a.at[pl.ds(0, planes - 1)], sum_send.at[0])
+    drain(sum_b.at[pl.ds(0, 7)], sum_send.at[1])
 
 
 def finish(factor_ref, first_ref, out_ref):
@@ -423,12 +478,10 @@
             pltpu.VMEM((orbits * 16, LANES), f32),
             pltpu.VMEM((orbits, 16 * LANES), f32),
             pltpu.VMEM((16, LANES), f32),
-            pltpu.VMEM((2, 8, 8, LANES), f32),
-            pltpu.VMEM((2, 8, 8, LANES), f32),
-            pltpu.VMEM((2, devices // 8, 8, LANES), f32),
-            pltpu.VMEM((2, 8, 8, LANES), f32),
+            pltpu.VMEM((devices // 8, 2, orbits // 2, 2 * orbits), f32),
+            pltpu.VMEM((8, 2, orbits // 2, 2 * orbits), f32),
             dma((4,)), dma((own,)), dma((own,)), dma((own,)), dma,
-            dma((2,)), dma((2,)), dma((2, 3)), dma((2, 3)),
+            dma((2,)), dma((2,)), dma((2,)), dma((2,)),
         ],
         compiler_params=pltpu.CompilerParams(
             collective_id=0, has_side_effects=True

time: 62.9 us -> 52.9 us (0.84)
  Pallas kernels: 62.8 us -> 52.7 us
    pallas_call x1, Pallas kernels: 60.3 us -> 50.3 us  [transposed(): pl.pallas_call(functools.partial(kernel, nx, ny), out_shape=(jax.ShapeDty...]
where the time goes in v5:
time: 52.9 us; the launch traced here: 52.7 us
  Pallas kernels  52.7 us (100%)
    pallas_call x1, Pallas kernels, transposed(): pl.pallas_call(functools.partial(kernel, nx, ny), out_shape=(jax.ShapeDty...  50.3 us
    pallas_call x1, Pallas kernels, transposed(): pl.pallas_call(finish, grid=(2,), out_shape=jax.ShapeDtypeStruct(psi.shap...  2.43 us

profile of v5, /device:TPU:0, one launch (start us, length us, event | category | flops | bytes accessed | tf_op | source)
XLA Modules:
  0.0 52.7 jit_solution(4586835349793831957)
XLA Ops:
  0.0 50.3 %shard_map.28 = (f32[64,2048]{1,0:T(8,128)}, f32[64,64]{1,0:T(8,128)}) custom-call(f32[64,8,256]{2,1,0:T(8,128)} %psi_ref.1, f32[8,256]{1,0:T(8,128)} %pot_ref.1), custom_call_target="tpu_custom_call" | custom-call | tf_op jit(solution)/shard_map/pallas_call | solution.py:462
  50.3 2.4 %shard_map.29 = f32[64,8,256]{2,1,0:T(8,128)} custom-call(f32[64,64]{1,0:T(8,128)} %get-tuple-element.7.factor_ref, f32[64,2048]{1,0:T(8,128)} %get-tuple-element.8.first_ref), custom_call_target="tpu_custom_call" | custom-call | tf_op jit(solution)/shard_map/pallas_call | solution.py:490

commit v6 on v5

--- a/solution.py
+++ b/solution.py
@@ -292,30 +292,25 @@
         here = pots.at[my_place, my_plane]
         copy_out(here, here, (pot_send.at[0], pot_recv.at[0]), plane_peer(step)).start()
 
-    stride = next(n for n in (13, 11, 7, 5, 3, 1) if math.gcd(n, devices) == 1)
-
-    def send_psi(o):
-        def body(i, _):
-            target = lax.rem(me + i * stride, devices)
-            copy_out(
-                send.at[target * own + o], field.at[o, me],
-                (psi_send.at[o], psi_recv.at[o]), target,
-            ).start()
-            return 0
-
-        lax.fori_loop(1, devices, body, 0)
-        field[o, me] = send[me * own + o]
-
     for c in loads[:2]:
         c.wait()
-    send_psi(0)
+
+    stride = next(n for n in (13, 11, 7, 5, 3, 1) if math.gcd(n, devices) == 1)
+
+    def send_psi(i, _):
+        target = lax.rem(me + i * stride, devices)
+        copy_out(
+            send.at[pl.ds(target * own, own)], field.at[me], (psi_send, psi_recv), target
+        ).start()
+        return 0
+
+    lax.fori_loop(1, devices, send_psi, 0)
+    field[me] = send[pl.ds(me * own, own)]
     drain(pots.at[0, pl.ds(0, planes - 1)], pot_recv.at[0])
     drain(pots.at[0, pl.ds(0, planes - 1)], pot_send.at[0])
     for step in range(1, 8):
         here = pots.at[my_place]
         copy_out(here, here, (pot_send.at[1], pot_recv.at[1]), place_peer(step)).start()
-    for o in range(1, own):
-        send_psi(o)
 
     zmat = z_matrix()
     tiles = 2 * ny
@@ -325,7 +320,7 @@
 
     def tile_of(ref, o, t):
         return jnp.concatenate(
-            [ref[o, b * ny + t // 2, 8 * (t % 2) : 8 * (t % 2) + 8, :] for b in range(nx)], axis=0
+            [ref[b * ny + t // 2, o, 8 * (t % 2) : 8 * (t % 2) + 8, :] for b in range(nx)], axis=0
         )
 
     def pot_tile(t):
@@ -364,8 +359,8 @@
         block[pl.ds((me * own + o) * 16, 16), :] = back[o, me]
 
     for o in range(own):
-        drain(field.at[o, pl.ds(0, devices - 1)], psi_recv.at[o])
         if o == 0:
+            drain(field.at[pl.ds(0, devices - 1)], psi_recv)
             drain(pots.at[pl.ds(0, 7)], pot_recv.at[1])
         for t in range(tiles):
             work[0, t] = tile_of(field, o, t)
@@ -392,32 +387,43 @@
         matrix[:, j * LANES : (j + 1) * LANES] = block[pl.ds(j, orbits, stride=16), :]
 
     ncount = float(rows * tiles * LANES)
-    upper = orbits // 2
+    mid = orbits // 2
+    lane = lax.broadcasted_iota(jnp.int32, (mid, 2 * orbits), 1)
 
     def total_gram(local):
-        low_lane = lax.broadcasted_iota(jnp.int32, (upper, 2 * orbits), 1) < orbits
-        for i in range(2):
-            sum_a[my_plane, i] = jnp.where(low_lane, local[i][:upper], local[i][upper:])
+        value, rest = local
+        corner = jnp.where(lane % orbits < mid, value[:mid], pltpu.roll(rest[:mid], mid, 1))
+        quarter = mid // 2
+        sum_a[my_plane, :mid] = jnp.where(lane < orbits, value[mid:], rest[mid:])
+        sum_a[my_plane, mid:] = jnp.where(lane[:quarter] < orbits, corner[:quarter], corner[quarter:])
+
+        def add_up(ref, count):
+            total = ref[0]
+            lost = jnp.zeros_like(total)
+            for i in range(1, count):
+                total, part = two_sum(total, ref[i])
+                lost = lost + part
+            first_part = jnp.where(lane >= orbits, pltpu.roll(lost[:mid], orbits, 1), 0.0)
+            second_part = jnp.where(lane[:quarter] % orbits >= mid, pltpu.roll(lost[mid:], mid, 1), 0.0)
+            return total + jnp.concatenate([first_part, second_part], axis=0)
+
         for step in range(1, planes):
             here = sum_a.at[my_plane]
             copy_out(here, here, (sum_send.at[0], sum_recv.at[0]), plane_peer(step)).start()
         drain(sum_a.at[pl.ds(0, planes - 1)], sum_recv.at[0])
-        total = sum_a[0, 0], sum_a[0, 1]
-        for i in range(1, planes):
-            total = pair_add(total, (sum_a[i, 0], sum_a[i, 1]))
-        for i in range(2):
-            sum_b[my_place, i] = total[i]
+        sum_b[my_place] = add_up(sum_a, planes)
         for step in range(1, 8):
             here = sum_b.at[my_place]
             copy_out(here, here, (sum_send.at[1], sum_recv.at[1]), place_peer(step)).start()
         drain(sum_b.at[pl.ds(0, 7)], sum_recv.at[1])
-        total = sum_b[0, 0], sum_b[0, 1]
-        for i in range(1, 8):
-            total = pair_add(total, (sum_b[i, 0], sum_b[i, 1]))
-        total = settle(total)
-        return [
-            jnp.concatenate([part, pltpu.roll(part, orbits, 1)], axis=0) * (1.0 / ncount) for part in total
-        ]
+        total = add_up(sum_b, 8) * (1.0 / ncount)
+        corner = jnp.concatenate([total[mid:], pltpu.roll(total[mid:], orbits, 1)], axis=0)
+        out = []
+        for lower, diagonal in ((total[:mid], corner), (pltpu.roll(total[:mid], orbits, 1), pltpu.roll(corner, 2 * orbits - mid, 1))):
+            square = jnp.concatenate([lower, jnp.zeros((2 * orbits - mid, 2 * orbits), jnp.float32)], axis=0)
+            across = pltpu.roll(square.T[:mid], mid, 1)
+            out.append(jnp.concatenate([jnp.where(lane < mid, diagonal, across), lower], axis=0))
+        return settle(out)
 
     def tiles_of(array):
         return [array[8 * i : 8 * i + 8] for i in range(orbits // 8)]
@@ -436,9 +442,9 @@
     factor_ref[...] = inverse_factor(tiles_of(second[0]))
 
     store.wait()
+    drain(field.at[pl.ds(0, devices - 1)], psi_send)
     drain(pots.at[pl.ds(0, 7)], pot_send.at[1])
     for o in range(own):
-        drain(field.at[o, pl.ds(0, devices - 1)], psi_send.at[o])
         drain(back.at[o, pl.ds(0, devices - 1)], ret_send.at[o])
     drain(sum_a.at[pl.ds(0, planes - 1)], sum_send.at[0])
     drain(sum_b.at[pl.ds(0, 7)], sum_send.at[1])
@@ -469,7 +475,7 @@
         out_specs=(pl.BlockSpec(memory_space=pl.ANY), pl.BlockSpec(memory_space=pltpu.VMEM)),
         scratch_shapes=[
             pltpu.VMEM((orbits, 16, LANES), f32),
-            pltpu.VMEM((own, devices, 16, LANES), f32),
+            pltpu.VMEM((devices, own, 16, LANES), f32),
             pltpu.VMEM((8, devices // 8, 16, LANES), f32),
             pltpu.VMEM((3, tiles, rows, LANES), f32),
             pltpu.VMEM((tiles, rows, LANES), f32),
@@ -478,9 +484,9 @@
             pltpu.VMEM((orbits * 16, LANES), f32),
             pltpu.VMEM((orbits, 16 * LANES), f32),
             pltpu.VMEM((16, LANES), f32),
-            pltpu.VMEM((devices // 8, 2, orbits // 2, 2 * orbits), f32),
-            pltpu.VMEM((8, 2, orbits // 2, 2 * orbits), f32),
-            dma((4,)), dma((own,)), dma((own,)), dma((own,)), dma,
+            pltpu.VMEM((devices // 8, 3 * orbits // 4, 2 * orbits), f32),
+            pltpu.VMEM((8, 3 * orbits // 4, 2 * orbits), f32),
+            dma((4,)), dma, dma, dma((own,)), dma,
             dma((2,)), dma((2,)), dma((2,)), dma((2,)),
         ],
         compiler_params=pltpu.CompilerParams(

time: 52.9 us -> 55.1 us (1.042)
  Pallas kernels: 52.7 us -> 55 us
    pallas_call x1, Pallas kernels: 50.3 us -> 52.5 us  [transposed(): pl.pallas_call(functools.partial(kernel, nx, ny), out_shape=(jax.ShapeDty...]
where the time goes in v6:
time: 55.1 us; the launch traced here: 55 us
  Pallas kernels  55 us (100%)
    pallas_call x1, Pallas kernels, transposed(): pl.pallas_call(functools.partial(kernel, nx, ny), out_shape=(jax.ShapeDty...  52.5 us
    pallas_call x1, Pallas kernels, transposed(): pl.pallas_call(finish, grid=(2,), out_shape=jax.ShapeDtypeStruct(psi.shap...  2.43 us

profile of v6, /device:TPU:0, one launch (start us, length us, event | category | flops | bytes accessed | tf_op | source)
XLA Modules:
  0.0 55.0 jit_solution(3282480740444853270)
XLA Ops:
  0.0 52.5 %shard_map.28 = (f32[64,2048]{1,0:T(8,128)}, f32[64,64]{1,0:T(8,128)}) custom-call(f32[64,8,256]{2,1,0:T(8,128)} %psi_ref.1, f32[8,256]{1,0:T(8,128)} %pot_ref.1), custom_call_target="tpu_custom_call" | custom-call | tf_op jit(solution)/shard_map/pallas_call | solution.py:468
  52.5 2.4 %shard_map.29 = f32[64,8,256]{2,1,0:T(8,128)} custom-call(f32[64,64]{1,0:T(8,128)} %get-tuple-element.7.factor_ref, f32[64,2048]{1,0:T(8,128)} %get-tuple-element.8.first_ref), custom_call_target="tpu_custom_call" | custom-call | tf_op jit(solution)/shard_map/pallas_call | solution.py:496
